TPU v7x, 32 devices: a whole 2x2x4 slice. The times are simulated.
32 devices in a mesh: row: 4 (over y, x), col: 8 (over z, core).
Axes of the slice: x: 2, y: 2, z: 4, core: 2. Of those that a mesh axis runs over, the one named last changes fastest.
Arguments:
- points: float32 [8, 4096], P(None, ('row', 'col')), may hold values from -6 to 6
- lengthscale: float32 [8], replicated, may hold values from 1.5 to 4
- signal_var: float32 [1], replicated, may hold values from 0.002 to 0.01
- noise_var: float32 [1], replicated, may hold values from 0.3 to 1.5
- solution: float32 [4, 4096], P(None, ('row', 'col')), may hold values from -6 to 6
- residual: float32 [4, 4096], P(None, ('row', 'col')), may hold values from -30 to 30, as said below
- direction: float32 [4, 4096], P(None, ('row', 'col')), may hold values from -6 to 6
Outputs:
- new_solution: float32 [4, 4096], P(None, ('row', 'col'))
- new_residual: float32 [4, 4096], P(None, ('row', 'col'))
- new_direction: float32 [4, 4096], P(None, ('row', 'col'))
Inputs may be any that keep to these rules, and one draw needn't show every extreme that they name: residual values, real-valued.
All inputs are finite; a program needn't handle non-finite values.
Results may differ from a plain program's by a relative error of at most 0.00017.
Values sent between devices are 32-bit elements; how exact they have to be, the bound alone decides.
A program may use at most 128 MiB of HBM per device.

v0:
```python
import jax
import jax.numpy as jnp
from jax import lax
from jax.sharding import PartitionSpec as P


def kernel_apply(row_pts, col_pts, col_dir, scale):
    rows = row_pts.shape[1]
    block = min(256, rows)
    blocks = row_pts.reshape(row_pts.shape[0], rows // block, block).transpose(1, 0, 2)

    def one_block(left):
        dist_sq = jnp.zeros((left.shape[1], col_pts.shape[1]), jnp.float32)
        for dim_idx in range(left.shape[0]):
            delta = left[dim_idx][:, None] - col_pts[dim_idx][None, :]
            dist_sq = dist_sq + delta * delta
        radius = jnp.sqrt(dist_sq)
        root_five = jnp.sqrt(jnp.float32(5.0))
        values = (
            scale * (1.0 + root_five * radius + 5.0 / 3.0 * dist_sq) * jnp.exp(-root_five * radius)
        )
        return jnp.einsum("rc,kc->kr", values, col_dir, precision=lax.Precision.HIGHEST)

    result = lax.map(one_block, blocks)
    return result.transpose(1, 0, 2).reshape(col_dir.shape[0], rows)


def on_device(points, lengthscale, signal_var, noise_var, solution, residual, direction):
    scaled = points / lengthscale[:, None]
    all_pts, all_dir = (
        lax.all_gather(scaled, ("row", "col"), axis=1, tiled=True),
        lax.all_gather(direction, ("row", "col"), axis=1, tiled=True),
    )
    applied = kernel_apply(scaled, all_pts, all_dir, signal_var[0])
    image = applied + noise_var[0] * direction
    old_rr = lax.psum(jnp.sum(residual * residual, axis=1), ("row", "col"))
    curv = lax.psum(jnp.sum(direction * image, axis=1), ("row", "col"))
    alpha = old_rr / curv
    new_solution = solution + alpha[:, None] * direction
    new_residual = residual - alpha[:, None] * image
    new_rr = lax.psum(jnp.sum(new_residual * new_residual, axis=1), ("row", "col"))
    new_direction = new_residual + (new_rr / old_rr)[:, None] * direction
    return (new_solution, new_residual, new_direction)


def solution(mesh):
    in_specs = (
        P(None, ("row", "col")),
        P(),
        P(),
        P(),
        P(None, ("row", "col")),
        P(None, ("row", "col")),
        P(None, ("row", "col")),
    )
    out_specs = (P(None, ("row", "col")), P(None, ("row", "col")), P(None, ("row", "col")))
    return jax.shard_map(
        on_device, mesh=mesh, in_specs=in_specs, out_specs=out_specs, check_vma=False
    )
```

profile of v0, /device:TPU:0, one launch (start us, length us, event | category | flops | bytes accessed | tf_op | source)
XLA Modules:
  0.0 167.7 jit_solution(3774342896621262591)
XLA Ops:
  0.6 0.8 broadcast_divide_fusion
  1.4 43.7 %all_gather.6 = f32[8,4096]{1,0:T(8,128)S(1)} all-gather(f32[8,128]{1,0:T(8,128)S(1)} %broadcast_divide_fusion), channel_id=1, replica_groups=mesh['row'=4,'col'=8] {'row','col'}, dimensions={1}, use_global_device_ids=true | all-gather | bytes 135168 | tf_op jit(solution)/shard_map/all_gather | solution.py:31
  45.1 0.0 copy-start.1
  45.1 0.1 fusion.64
  45.2 0.6 copy-done.1
  45.8 36.9 %all_gather.7 = f32[4,4096]{1,0:T(4,128)S(1)} all-gather(f32[4,128]{1,0:T(4,128)S(1)} %copy-done.1), channel_id=1, replica_groups=mesh['row'=4,'col'=8] {'row','col'}, dimensions={1}, use_global_device_ids=true | all-gather | bytes 67584 | tf_op jit(solution)/shard_map/all_gather | solution.py:32
  84.0 0.0 copy-start
  84.0 0.0 copy-start.3
  84.0 4.5 %multiply_reduce_fusion.1 = (f32[4]{0:T(128)S(1)}, f32[4,128]{1,0:T(4,128)S(1)}) fusion(f32[4,128]{1,0:T(4,128)S(1)} %copy-done.1, f32[]{:T(128)} %bitcast.32, f32[4,4096]{1,0:T(4,128)S(1)} %all_gather.7, f32[4096]{0:T(1024)S(1)} %bitcast.34, f32[128]{0:T(128)S(1)} %get-tuple-element.34, f32[4096]{0:T(1024)S(1)} %bitcast.35, f32[128]{0:T(128)S(1)} %get-tuple-element.35, ...), kind=kOutput, calls=%fused_computation.60 | convolution fusion | flops 40896508 | bytes 204824 | tf_op jit(solution)/shard_map/while/body/eval_jaxpr/rc,kc->kr/dot_general | solution.py:22
  88.5 0.0 copy-done
  88.5 0.1 multiply_reduce_fusion.2
  88.6 39.4 %all-reduce = (f32[4]{0:T(128)S(1)}, f32[4]{0:T(128)S(1)}) all-reduce(f32[4]{0:T(128)S(1)} %multiply_reduce_fusion.2, f32[4]{0:T(128)S(1)} %get-tuple-element.43), channel_id=1, replica_groups=mesh['row'=4,'col'=8] {'row','col'}, use_global_device_ids=true, to_apply=%region_1.2 | all-reduce | flops 8 | bytes 64 | tf_op jit(solution)/shard_map/psum | solution.py:36
  128.0 0.2 multiply_reduce_fusion
  128.2 0.0 copy-start.2
  128.2 38.9 %psum.23 = f32[4]{0:T(128)S(1)} all-reduce(f32[4]{0:T(128)S(1)} %get-tuple-element.17), channel_id=1, replica_groups=mesh['row'=4,'col'=8] {'row','col'}, use_global_device_ids=true, to_apply=%region_5.6 | all-reduce | flops 4 | bytes 32 | tf_op jit(solution)/shard_map/psum | solution.py:41
  167.0 0.0 copy-done.3
  167.0 0.7 multiply_add_fusion
  167.7 0.0 copy-done.2
  (3 shorter events, 0.0 us)
Async XLA Ops:
  45.1 0.7 copy-start.1
  84.0 4.5 %copy-start = (f32[4,128]{1,0:T(4,128)S(1)}, f32[4,128]{1,0:T(4,128)}, u32[]{:S(2)}) copy-start(f32[4,128]{1,0:T(4,128)} %param.12) | copy-start | bytes 6148
  84.0 83.1 %copy-start.3 = (f32[4,128]{1,0:T(4,128)S(1)}, f32[4,128]{1,0:T(4,128)}, u32[]{:S(2)}) copy-start(f32[4,128]{1,0:T(4,128)} %param.11) | copy-start | bytes 6148
  128.2 39.5 %copy-start.2 = (f32[4,128]{1,0:T(4,128)}, f32[4,128]{1,0:T(4,128)S(1)}, u32[]{:S(2)}) copy-start(f32[4,128]{1,0:T(4,128)S(1)} %get-tuple-element.24) | copy-start | bytes 6148
where the time goes:
time: 168 us
  blocking collectives  159 us (95%)
  matrix products  4.45 us (3%)
  between operations  1.98 us (1%)
  other arithmetic  1.73 us (1%)
    all_gather x1, blocking collectives, on_device(): lax.all_gather(scaled, ('row', 'col'), axis=1, tiled=True)  43.7 us
    psum x1, blocking collectives, on_device(): old_rr = lax.psum(jnp.sum(residual * residual, axis=1), ('row', 'col'))  39.4 us
    psum x1, blocking collectives, on_device(): lax.psum(jnp.sum(new_residual * new_residual, axis=1), ('row', 'col'))  38.9 us
    all_gather x1, blocking collectives, on_device(): lax.all_gather(direction, ('row', 'col'), axis=1, tiled=True)  36.9 us
    dot_general x1, matrix products, one_block(): jnp.einsum('rc,kc->kr', values, col_dir, precision=lax.Precision.HIGHEST)  4.45 us

commit v1 on v0

v1 whole, which is shorter than its diff:
```python
import functools
import math

import jax
import jax.numpy as jnp
from jax import lax
from jax.experimental import pallas as pl
from jax.experimental.pallas import tpu as pltpu
from jax.sharding import PartitionSpec as P

MESH = pl.DeviceIdType.MESH
F32 = jnp.float32
BF16 = jnp.bfloat16
LN2 = math.log(2.0)
STEP = math.sqrt(5.0) / LN2
SLOTS = 4


def split3(x):
    a = x.astype(BF16).astype(F32)
    rest = x - a
    b = rest.astype(BF16).astype(F32)
    c = (rest - b).astype(BF16).astype(F32)
    return a, b, c


def norm_rows(x, first):
    n1, n2, n3 = split3(jnp.sum(x * x, axis=0, keepdims=True))
    row = lax.broadcasted_iota(jnp.int32, x.shape, 0)
    base = 0 if first else 3
    ones = (row >= 3 - base) & (row < 6 - base)
    out = jnp.where(ones, 1.0, 0.0)
    for i, part in enumerate((n1, n2, n3)):
        out = jnp.where(row == base + i, part, out)
    return out


def left_rows(x):
    a, b, c = split3(x)
    rows = [-2.0 * v for v in (a, a, b, b, a, c)]
    return jnp.concatenate(rows + [norm_rows(x, False), jnp.zeros_like(x)], axis=0)


def right_rows(x):
    a, b, c = split3(x)
    return jnp.concatenate([a, b, a, b, c, a, norm_rows(x, True), jnp.zeros_like(x)], axis=0)


def cg_kernel(rows, cols, len_ref, sig_ref, noise_ref, pts_ref, sol_ref, res_ref, dir_ref,
              nsol_ref, nres_ref, ndir_ref, held, sums, send_sem, recv_sem, sum_send, sum_recv):
    n = rows * cols
    me = lax.axis_index("row") * cols + lax.axis_index("col")
    dims, width = pts_ref.shape
    rhs = dir_ref.shape[0]

    def peer_of(k):
        peer = lax.rem(me + k, n)
        return (peer // cols, lax.rem(peer, cols))

    barrier = pltpu.get_barrier_semaphore()

    @pl.loop(1, n)
    def _(k):
        pl.semaphore_signal(barrier, inc=1, device_id=peer_of(k), device_id_type=MESH)

    held[me, :, 0:width] = pts_ref[0:rhs, :]
    held[me, :, width:2 * width] = pts_ref[rhs:dims, :]
    held[me, :, 2 * width:] = dir_ref[...]
    pl.semaphore_wait(barrier, n - 1)

    @pl.loop(1, n)
    def _(k):
        pltpu.make_async_remote_copy(
            src_ref=held.at[me], dst_ref=held.at[me], send_sem=send_sem, recv_sem=recv_sem,
            device_id=peer_of(k), device_id_type=MESH).start()

    row = lax.broadcasted_iota(jnp.int32, (dims, width), 0)
    scale = jnp.zeros((dims, width), F32)
    for i in range(dims):
        scale = jnp.where(row == i, len_ref[i], scale)
    scale = STEP / scale
    left = left_rows(pts_ref[...] * scale).T.astype(BF16)
    direction = dir_ref[...]
    residual = res_ref[...]

    pltpu.make_async_copy(held.at[pl.ds(0, n - 1)], held.at[pl.ds(0, n - 1)], recv_sem).wait()

    def chunk(c, total):
        right, dirs = [], []
        for j in range(SLOTS):
            block = held[c * SLOTS + j]
            x = jnp.concatenate([block[:, 0:width], block[:, width:2 * width]], axis=0)
            right.append(right_rows(x * scale))
            dirs.append(block[:, 2 * width:])
        right = jnp.concatenate(right, axis=1).astype(BF16)
        dirs = jnp.concatenate(dirs, axis=1)
        d1, d2, d3 = split3(dirs)
        dirs = jnp.concatenate([d1, d2, d3, jnp.zeros_like(d1)], axis=0).astype(BF16)
        v = jnp.maximum(jnp.dot(left, right, preferred_element_type=F32), 1e-30)
        w = v * lax.rsqrt(v)
        k = (1.0 + LN2 * w + (LN2 * LN2 / 3.0) * v) * jnp.exp2(-w)
        k1 = k.astype(BF16)
        k2 = (k - k1.astype(F32)).astype(BF16)
        nt = (((1,), (1,)), ((), ()))
        return (total + lax.dot_general(k1, dirs, nt, preferred_element_type=F32)
                + lax.dot_general(k2, dirs, nt, preferred_element_type=F32))

    total = lax.fori_loop(0, n // SLOTS, chunk, jnp.zeros((width, 4 * rhs), F32))
    total = total.T
    total = total[0:rhs] + total[rhs:2 * rhs] + total[2 * rhs:3 * rhs]
    image = sig_ref[0] * total + noise_ref[0] * direction

    def over(x):
        return jnp.sum(x, axis=1, keepdims=True)

    dq, rr, rq, qq = over(direction * image), over(residual * residual), over(residual * image), over(image * image)
    fits = qq > 1e-30
    near = jnp.where(fits, rq / jnp.where(fits, qq, 1.0), 0.0)
    left_over = residual - near * image
    pq, pp = over(left_over * image), over(left_over * left_over)
    lane = lax.broadcasted_iota(jnp.int32, (rhs, width), 1)
    sub = lax.broadcasted_iota(jnp.int32, (rhs, width), 0)
    mine = jnp.zeros((rhs, width), F32)
    for i, part in enumerate((dq, rr, near, qq, pq, pp)):
        mine = jnp.where(lane == sub + i * rhs, part, mine)
    sums[me] = jnp.sum(mine, axis=0, keepdims=True)

    @pl.loop(1, n)
    def _(k):
        pltpu.make_async_remote_copy(
            src_ref=sums.at[me], dst_ref=sums.at[me], send_sem=sum_send, recv_sem=sum_recv,
            device_id=peer_of(k), device_id_type=MESH).start()

    pltpu.make_async_copy(held.at[pl.ds(0, n - 1)], held.at[pl.ds(0, n - 1)], send_sem).wait()
    pltpu.make_async_copy(sums.at[pl.ds(0, n - 1)], sums.at[pl.ds(0, n - 1)], sum_recv).wait()

    every = sums[:, 0, :]

    def part(x, i):
        return x if i == 0 else pltpu.roll(x, width - i * rhs, 1)

    whole = jnp.sum(every, axis=0, keepdims=True)
    all_rr = jnp.sum(part(every, 1), axis=0, keepdims=True)
    used = lax.broadcasted_iota(jnp.int32, (1, width), 1) < rhs
    alpha = all_rr / jnp.where(used, whole, 1.0)
    off = alpha - part(every, 2)
    new_rr = jnp.sum(part(every, 5) + off * (off * part(every, 3) - 2.0 * part(every, 4)), axis=0, keepdims=True)
    beta = new_rr / jnp.where(used, all_rr, 1.0)
    diag = lane == sub
    alpha = over(jnp.where(diag, alpha, 0.0))
    beta = over(jnp.where(diag, beta, 0.0))
    nsol_ref[...] = sol_ref[...] + alpha * direction
    new_residual = residual - alpha * image
    nres_ref[...] = new_residual
    ndir_ref[...] = new_residual + beta * direction
    pltpu.make_async_copy(sums.at[pl.ds(0, n - 1)], sums.at[pl.ds(0, n - 1)], sum_send).wait()


def solution(mesh):
    rows, cols = mesh.shape["row"], mesh.shape["col"]
    n = rows * cols

    def on_device(points, lengthscale, signal_var, noise_var, solution, residual, direction):
        rhs, width = direction.shape
        vmem = pl.BlockSpec(memory_space=pltpu.VMEM)
        smem = pl.BlockSpec(memory_space=pltpu.SMEM)
        out = jax.ShapeDtypeStruct((rhs, width), F32)
        return pl.pallas_call(
            functools.partial(cg_kernel, rows, cols),
            out_shape=(out, out, out),
            in_specs=[smem] * 3 + [vmem] * 4,
            out_specs=(vmem, vmem, vmem),
            scratch_shapes=[
                pltpu.VMEM((n, rhs, 3 * width), F32),
                pltpu.VMEM((n, 1, width), F32),
                pltpu.SemaphoreType.DMA,
                pltpu.SemaphoreType.DMA,
                pltpu.SemaphoreType.DMA,
                pltpu.SemaphoreType.DMA,
            ],
            compiler_params=pltpu.CompilerParams(
                collective_id=0, has_side_effects=True, vmem_limit_bytes=32 * 1024 * 1024),
            cost_estimate=pl.CostEstimate(
                flops=2 * 80 * n * width * width, bytes_accessed=32 * 1024,
                transcendentals=2 * n * width * width),
        )(lengthscale, signal_var, noise_var, points, solution, residual, direction)

    spread = P(None, ("row", "col"))
    return jax.shard_map(
        on_device, mesh=mesh, in_specs=(spread, P(), P(), P(), spread, spread, spread),
        out_specs=(spread, spread, spread), check_vma=False)
```

time: 168 us -> 28.8 us (0.17)
  blocking collectives: 159 us -> 0 us
  Pallas kernels: 0 us -> 22.8 us
  matrix products: 4.45 us -> 0 us
  local copies, waits for them, and re-layouts: 0.69 us -> 3.79 us
  other arithmetic: 1.73 us -> 0 us
    all_gather x2 -> x0, blocking collectives: 80.6 us -> none  [the longest x1 43.7 us: on_device(): lax.all_gather(scaled, ('row', 'col'), axis=1, tiled=True)]
    psum x2 -> x0, blocking collectives: 78.2 us -> none  [the longest x1 39.4 us: on_device(): old_rr = lax.psum(jnp.sum(residual * residual, axis=1), ('row', 'col'))]
    pallas_call x0 -> x1, Pallas kernels: none -> 22.8 us  [on_device(): pl.pallas_call(functools.partial(cg_kernel, rows, cols), out_shape=(out,...]
    dot_general x1 -> x0, matrix products: 4.45 us -> none  [one_block(): jnp.einsum('rc,kc->kr', values, col_dir, precision=lax.Precision.HIGHEST)]
    unnamed x8 -> x13, local copies, waits for them, and re-layouts: 0.59 us -> 3.79 us
where the time goes in v1:
time: 28.8 us; the launch traced here: 28.6 us
  Pallas kernels  22.8 us (79%)
  local copies, waits for them, and re-layouts  3.79 us (13%)
  between operations  2 us (7%)
    pallas_call x1, Pallas kernels, on_device(): pl.pallas_call(functools.partial(cg_kernel, rows, cols), out_shape=(out,...  22.8 us
    unnamed x13, local copies, waits for them, and re-layouts  3.79 us

profile of v1, /device:TPU:0, one launch (start us, length us, event | category | flops | bytes accessed | tf_op | source)
XLA Modules:
  0.0 28.6 jit_solution(14421681680792877224)
XLA Ops:
  0.6 0.0 copy-start.1
  1.3 0.0 copy-start.4
  2.0 0.0 copy-done.1
  2.0 0.0 copy-done.4
  2.0 0.0 copy-start
  2.0 0.7 %copy-done = f32[8,128]{1,0:T(8,128)S(1)} copy-done((f32[8,128]{1,0:T(8,128)S(1)}, f32[8,128]{1,0:T(8,128)}, u32[]{:S(2)}) %copy-start) | copy-done | bytes 4120
  2.7 0.0 copy-start.2
  2.7 0.7 %copy-done.2 = f32[4,128]{1,0:T(4,128)S(1)} copy-done((f32[4,128]{1,0:T(4,128)S(1)}, f32[4,128]{1,0:T(4,128)}, u32[]{:S(2)}) %copy-start.2) | copy-done | bytes 2072
  3.4 0.0 copy-start.3
  3.4 0.7 %copy-done.3 = f32[4,128]{1,0:T(4,128)S(1)} copy-done((f32[4,128]{1,0:T(4,128)S(1)}, f32[4,128]{1,0:T(4,128)}, u32[]{:S(2)}) %copy-start.3) | copy-done | bytes 2072
  4.0 22.8 %shard_map.94 = (f32[4,128]{1,0:T(4,128)S(1)}, f32[4,128]{1,0:T(4,128)S(1)}, f32[4,128]{1,0:T(4,128)S(1)}) custom-call(f32[8]{0:T(128)S(1)} %copy-done.4, f32[1]{0:T(128)S(6)} %copy.13.sig_ref, f32[1]{0:T(128)S(6)} %copy.14.noise_ref, f32[8,128]{1,0:T(8,128)S(1)} %copy-done, f32[4,128]{1,0:T(4,128)S(1)} %copy-done.1, f32[4,128]{1,0:T(4,128)S(1)} %copy-done.2, ...), custom_call_target="tpu_custom_call" | custom-call | flops 83886080 | bytes 32768 | tf_op jit(solution)/shard_map/pallas_call | solution.py:168
  26.8 0.6 %copy.15 = f32[4,128]{1,0:T(4,128)} copy(f32[4,128]{1,0:T(4,128)S(1)} %get-tuple-element.6) | data formatting | bytes 4096
  27.4 0.6 %copy.16 = f32[4,128]{1,0:T(4,128)} copy(f32[4,128]{1,0:T(4,128)S(1)} %get-tuple-element.7) | data formatting | bytes 4096
  28.0 0.6 %copy.17 = f32[4,128]{1,0:T(4,128)} copy(f32[4,128]{1,0:T(4,128)S(1)} %get-tuple-element.8) | data formatting | bytes 4096
Async XLA Ops:
  0.6 1.3 %copy-start.1 = (f32[4,128]{1,0:T(4,128)S(1)}, f32[4,128]{1,0:T(4,128)}, u32[]{:S(2)}) copy-start(f32[4,128]{1,0:T(4,128)} %sol_ref.1) | copy-start | bytes 6148
  1.3 0.7 %copy-start.4 = (f32[8]{0:T(128)S(1)}, f32[8]{0:T(128)}, u32[]{:S(2)}) copy-start(f32[8]{0:T(128)} %len_ref.1) | copy-start | bytes 100
  2.0 0.7 %copy-start = (f32[8,128]{1,0:T(8,128)S(1)}, f32[8,128]{1,0:T(8,128)}, u32[]{:S(2)}) copy-start(f32[8,128]{1,0:T(8,128)} %pts_ref.1) | copy-start | bytes 12292
  2.7 0.7 %copy-start.2 = (f32[4,128]{1,0:T(4,128)S(1)}, f32[4,128]{1,0:T(4,128)}, u32[]{:S(2)}) copy-start(f32[4,128]{1,0:T(4,128)} %res_ref.1) | copy-start | bytes 6148
  3.4 0.7 %copy-start.3 = (f32[4,128]{1,0:T(4,128)S(1)}, f32[4,128]{1,0:T(4,128)}, u32[]{:S(2)}) copy-start(f32[4,128]{1,0:T(4,128)} %dir_ref.1) | copy-start | bytes 6148

commit v2 on v1

v2 whole, which is shorter than its diff:
```python
import functools
import math

import jax
import jax.numpy as jnp
from jax import lax
from jax.experimental import pallas as pl
from jax.experimental.pallas import tpu as pltpu
from jax.sharding import PartitionSpec as P

MESH = pl.DeviceIdType.MESH
F32 = jnp.float32
BF16 = jnp.bfloat16
LN2 = math.log(2.0)
STEP = math.sqrt(5.0) / LN2


def split3(x):
    a = x.astype(BF16).astype(F32)
    rest = x - a
    b = rest.astype(BF16).astype(F32)
    c = (rest - b).astype(BF16).astype(F32)
    return a, b, c


def norm_rows(x, first):
    n1, n2, n3 = split3(jnp.sum(x * x, axis=0, keepdims=True))
    row = lax.broadcasted_iota(jnp.int32, x.shape, 0)
    base = 0 if first else 3
    ones = (row >= 3 - base) & (row < 6 - base)
    out = jnp.where(ones, 1.0, 0.0)
    for i, part in enumerate((n1, n2, n3)):
        out = jnp.where(row == base + i, part, out)
    return out


def left_rows(x):
    a, b, c = split3(x)
    rows = [-2.0 * v for v in (a, a, b, b, a, c)]
    return jnp.concatenate(rows + [norm_rows(x, False), jnp.zeros_like(x)], axis=0)


def right_rows(x):
    a, b, c = split3(x)
    return jnp.concatenate([a, b, a, b, c, a, norm_rows(x, True), jnp.zeros_like(x)], axis=0)


def each(low, high, body):
    if high - low < 32:
        for k in range(low, high):
            body(k)
    else:
        pl.loop(low, high)(body)


def cg_kernel(rows, cols, len_hbm, sig_hbm, noise_hbm, pts_hbm, res_hbm, dir_hbm,
              move_ref,
              len_ref, sig_ref, noise_ref, res_ref, row_pts, col_all, made, got, sums, in_sem,
              pts_send, pts_recv, all_send, all_recv, part_send, part_recv, sum_send, sum_recv):
    n = rows * cols
    my_row, my_col = lax.axis_index("row"), lax.axis_index("col")
    me = my_row * cols + my_col
    _, dims, width = row_pts.shape
    rhs = res_ref.shape[0]

    def along(k):
        return lax.rem(my_col + k, cols)

    def across(k):
        return lax.rem(my_row + k, rows)

    def anyone(k):
        peer = lax.rem(me + k, n)
        return (peer // cols, lax.rem(peer, cols))

    mine_in = [
        pltpu.make_async_copy(pts_hbm, row_pts.at[my_col], in_sem.at[0]),
        pltpu.make_async_copy(dir_hbm, col_all.at[my_row, :, pl.ds(2 * width, width)], in_sem.at[1]),
        pltpu.make_async_copy(len_hbm, len_ref, in_sem.at[2]),
        pltpu.make_async_copy(res_hbm, res_ref, in_sem.at[3]),
        pltpu.make_async_copy(sig_hbm, sig_ref, in_sem.at[4]),
        pltpu.make_async_copy(noise_hbm, noise_ref, in_sem.at[5]),
    ]
    for copy in mine_in:
        copy.start()

    barrier = pltpu.get_barrier_semaphore()

    def greet(k):
        pl.semaphore_signal(barrier, inc=1, device_id=anyone(k), device_id_type=MESH)

    each(1, n, greet)
    mine_in[0].wait()
    mine_in[1].wait()
    points = row_pts[my_col]
    col_all[my_row, :, 0:width] = points[0:rhs]
    col_all[my_row, :, width:2 * width] = points[rhs:dims]
    pl.semaphore_wait(barrier, n - 1)

    def send_all(k):
        pltpu.make_async_remote_copy(
            src_ref=col_all.at[my_row], dst_ref=col_all.at[my_row], send_sem=all_send,
            recv_sem=all_recv, device_id=(across(k), my_col), device_id_type=MESH).start()

    def send_pts(k):
        pltpu.make_async_remote_copy(
            src_ref=row_pts.at[my_col], dst_ref=row_pts.at[my_col], send_sem=pts_send,
            recv_sem=pts_recv, device_id=(my_row, along(k)), device_id_type=MESH).start()

    each(1, rows, send_all)
    each(1, cols, send_pts)

    for copy in mine_in[2:]:
        copy.wait()
    row = lax.broadcasted_iota(jnp.int32, (dims, width), 0)
    scale = jnp.zeros((dims, width), F32)
    for i in range(dims):
        scale = jnp.where(row == i, len_ref[i], scale)
    scale = STEP / scale
    residual = res_ref[...]
    direction = col_all[my_row, :, 2 * width:]

    def wait_bytes(ref, count, sem):
        pltpu.make_async_copy(ref.at[pl.ds(0, count)], ref.at[pl.ds(0, count)], sem).wait()

    wait_bytes(col_all, rows - 1, all_recv)
    right, dirs = [], []
    for j in range(rows):
        block = col_all[j]
        x = jnp.concatenate([block[:, 0:width], block[:, width:2 * width]], axis=0)
        right.append(right_rows(x * scale))
        dirs.append(block[:, 2 * width:])
    right = jnp.concatenate(right, axis=1).astype(BF16)
    d1, d2, d3 = split3(jnp.concatenate(dirs, axis=1))
    dirs = jnp.concatenate([d1, d2, d3, jnp.zeros_like(d1)], axis=0).astype(BF16)
    wait_bytes(row_pts, cols - 1, pts_recv)

    def slab(k):
        to = along(k)
        left = left_rows(row_pts[to] * scale).T.astype(BF16)
        v = jnp.maximum(jnp.dot(left, right, preferred_element_type=F32), 1e-30)
        w = v * lax.rsqrt(v)
        kern = (1.0 + LN2 * w + (LN2 * LN2 / 3.0) * v) * jnp.exp2(-w)
        k1 = kern.astype(BF16)
        k2 = (kern - k1.astype(F32)).astype(BF16)
        nt = (((1,), (1,)), ((), ()))
        total = (lax.dot_general(k1, dirs, nt, preferred_element_type=F32)
                 + lax.dot_general(k2, dirs, nt, preferred_element_type=F32)).T
        return to, total[0:rhs] + total[rhs:2 * rhs] + total[2 * rhs:3 * rhs]

    def send_part(k):
        to, total = slab(k)
        made[to] = total
        pltpu.make_async_remote_copy(
            src_ref=made.at[to], dst_ref=got.at[my_col], send_sem=part_send, recv_sem=part_recv,
            device_id=(my_row, to), device_id_type=MESH).start()

    each(1, cols, send_part)
    got[my_col] = slab(0)[1]
    wait_bytes(got, cols - 1, part_recv)
    image = sig_ref[0, 0] * jnp.sum(got[...], axis=0) + noise_ref[0, 0] * direction

    def over(x):
        return jnp.sum(x, axis=1, keepdims=True)

    dq, rr, rq, qq = over(direction * image), over(residual * residual), over(residual * image), over(image * image)
    fits = qq > 1e-30
    near = jnp.where(fits, rq / jnp.where(fits, qq, 1.0), 0.0)
    left_over = residual - near * image
    pq, pp = over(left_over * image), over(left_over * left_over)
    lane = lax.broadcasted_iota(jnp.int32, (rhs, width), 1)
    sub = lax.broadcasted_iota(jnp.int32, (rhs, width), 0)
    mine = jnp.zeros((rhs, width), F32)
    for i, part in enumerate((dq, rr, near, qq, pq, pp)):
        mine = jnp.where(lane == sub + i * rhs, part, mine)
    sums[me] = jnp.sum(mine, axis=0, keepdims=True)

    def send_sum(k):
        pltpu.make_async_remote_copy(
            src_ref=sums.at[me], dst_ref=sums.at[me], send_sem=sum_send, recv_sem=sum_recv,
            device_id=anyone(k), device_id_type=MESH).start()

    each(1, n, send_sum)
    wait_bytes(col_all, rows - 1, all_send)
    wait_bytes(row_pts, cols - 1, pts_send)
    wait_bytes(made, cols - 1, part_send)
    wait_bytes(sums, n - 1, sum_recv)

    every = sums[:, 0, :]

    def part(x, i):
        return x if i == 0 else pltpu.roll(x, width - i * rhs, 1)

    whole = jnp.sum(every, axis=0, keepdims=True)
    all_rr = jnp.sum(part(every, 1), axis=0, keepdims=True)
    used = lax.broadcasted_iota(jnp.int32, (1, width), 1) < rhs
    alpha = all_rr / jnp.where(used, whole, 1.0)
    off = alpha - part(every, 2)
    new_rr = jnp.sum(part(every, 5) + off * (off * part(every, 3) - 2.0 * part(every, 4)), axis=0, keepdims=True)
    beta = new_rr / jnp.where(used, all_rr, 1.0)
    diag = lane == sub
    alpha = over(jnp.where(diag, alpha, 0.0))
    beta = over(jnp.where(diag, beta, 0.0))
    move_ref[0] = alpha * direction
    move_ref[1] = alpha * image
    move_ref[2] = beta * direction
    wait_bytes(sums, n - 1, sum_send)


def solution(mesh):
    rows, cols = mesh.shape["row"], mesh.shape["col"]
    n = rows * cols

    def on_device(points, lengthscale, signal_var, noise_var, solution, residual, direction):
        rhs, width = direction.shape
        dims = points.shape[0]
        vmem = pl.BlockSpec(memory_space=pltpu.VMEM)
        hbm = pl.BlockSpec(memory_space=pltpu.HBM)
        move = pl.pallas_call(
            functools.partial(cg_kernel, rows, cols),
            out_shape=jax.ShapeDtypeStruct((3, rhs, width), F32),
            in_specs=[hbm] * 6,
            out_specs=vmem,
            scratch_shapes=[
                pltpu.SMEM((dims,), F32),
                pltpu.SMEM((1, 1), F32),
                pltpu.SMEM((1, 1), F32),
                pltpu.VMEM((rhs, width), F32),
                pltpu.VMEM((cols, dims, width), F32),
                pltpu.VMEM((rows, rhs, 3 * width), F32),
                pltpu.VMEM((cols, rhs, width), F32),
                pltpu.VMEM((cols, rhs, width), F32),
                pltpu.VMEM((n, 1, width), F32),
                pltpu.SemaphoreType.DMA((6,)),
            ] + [pltpu.SemaphoreType.DMA] * 8,
            compiler_params=pltpu.CompilerParams(
                collective_id=0, has_side_effects=True, vmem_limit_bytes=60 * 1024 * 1024),
            cost_estimate=pl.CostEstimate(
                flops=2 * 80 * n * width * width, bytes_accessed=32 * 1024,
                transcendentals=2 * n * width * width),
        )(lengthscale, signal_var.reshape(1, 1), noise_var.reshape(1, 1), points, residual, direction)
        new_residual = residual - move[1]
        return solution + move[0], new_residual, new_residual + move[2]

    spread = P(None, ("row", "col"))
    return jax.shard_map(
        on_device, mesh=mesh, in_specs=(spread, P(), P(), P(), spread, spread, spread),
        out_specs=(spread, spread, spread), check_vma=False)
```

time: 28.8 us -> 25.7 us (0.89)
  local copies, waits for them, and re-layouts: 3.79 us -> 0.01 us
  other arithmetic: 0 us -> 1.28 us
  Pallas kernels: 22.8 us -> 22.3 us
    unnamed x13 -> x4, local copies, waits for them, and re-layouts: 3.79 us -> 0.01 us
    add x0 -> x1, other arithmetic: none -> 1.28 us  [on_device(): return (solution + move[0], new_residual, new_residual + move[2])]
    pallas_call x1, Pallas kernels: 22.8 us -> 22.3 us  [on_device(): pl.pallas_call(functools.partial(cg_kernel, rows, cols), out_shape=jax.Sh...]
where the time goes in v2:
time: 25.7 us; the launch traced here: 25.5 us
  Pallas kernels  22.3 us (87%)
  between operations  1.96 us (8%)
  other arithmetic  1.28 us (5%)
    pallas_call x1, Pallas kernels, on_device(): pl.pallas_call(functools.partial(cg_kernel, rows, cols), out_shape=jax.Sh...  22.3 us
    add x1, other arithmetic, on_device(): return (solution + move[0], new_residual, new_residual + move[2])  1.28 us

profile of v2, /device:TPU:0, one launch (start us, length us, event | category | flops | bytes accessed | tf_op | source)
XLA Modules:
  0.0 25.5 jit_solution(7979747636902030040)
XLA Ops:
  1.9 0.0 copy-start
  1.9 0.0 copy-start.1
  1.9 22.3 %shard_map.94 = f32[3,4,128]{2,1,0:T(4,128)} custom-call(f32[8]{0:T(128)} %len_hbm.1, f32[1,1]{1,0:T(1,128)} %bitcast.9.sig_hbm, f32[1,1]{1,0:T(1,128)} %bitcast.10.noise_hbm, f32[8,128]{1,0:T(8,128)} %pts_hbm.1, f32[4,128]{1,0:T(4,128)} %res_hbm.1, f32[4,128]{1,0:T(4,128)} %dir_hbm.1), custom_call_target="tpu_custom_call" | custom-call | flops 83886080 | bytes 32768 | tf_op jit(solution)/shard_map/pallas_call | solution.py:219
  24.2 0.0 copy-done
  24.3 0.0 copy-done.1
  24.3 1.3 %bitcast_add_fusion = (f32[4,128]{1,0:T(4,128)}, f32[4,128]{1,0:T(4,128)}, f32[4,128]{1,0:T(4,128)}) fusion(f32[3,4,128]{2,1,0:T(4,128)} %shard_map.94, f32[4,128]{1,0:T(4,128)S(1)} %copy-done, f32[4,128]{1,0:T(4,128)S(1)} %copy-done.1), kind=kLoop, calls=%fused_computation | loop fusion | flops 1536 | bytes 16384 | tf_op jit(solution)/shard_map/add | solution.py:243
Async XLA Ops:
  1.9 22.3 %copy-start = (f32[4,128]{1,0:T(4,128)S(1)}, f32[4,128]{1,0:T(4,128)}, u32[]{:S(2)}) copy-start(f32[4,128]{1,0:T(4,128)} %res_hbm.1) | copy-start | bytes 6148
  1.9 22.3 %copy-start.1 = (f32[4,128]{1,0:T(4,128)S(1)}, f32[4,128]{1,0:T(4,128)}, u32[]{:S(2)}) copy-start(f32[4,128]{1,0:T(4,128)} %param.11) | copy-start | bytes 6148

commit v3 on v2

v3 whole, which is shorter than its diff:
```python
import functools
import math

import jax
import jax.numpy as jnp
from jax import lax
from jax.experimental import pallas as pl
from jax.experimental.pallas import tpu as pltpu
from jax.sharding import PartitionSpec as P

MESH = pl.DeviceIdType.MESH
F32 = jnp.float32
BF16 = jnp.bfloat16
LN2 = math.log(2.0)
STEP = math.sqrt(5.0) / LN2


def split3(x):
    a = x.astype(BF16).astype(F32)
    rest = x - a
    b = rest.astype(BF16).astype(F32)
    c = (rest - b).astype(BF16).astype(F32)
    return a, b, c


def norm_rows(x, first):
    n1, n2, n3 = split3(jnp.sum(x * x, axis=0, keepdims=True))
    row = lax.broadcasted_iota(jnp.int32, x.shape, 0)
    base = 0 if first else 3
    ones = (row >= 3 - base) & (row < 6 - base)
    out = jnp.where(ones, 1.0, 0.0)
    for i, part in enumerate((n1, n2, n3)):
        out = jnp.where(row == base + i, part, out)
    return out


def left_rows(x):
    a, b, c = split3(x)
    rows = [-2.0 * v for v in (a, a, b, b, a, c)]
    return jnp.concatenate(rows + [norm_rows(x, False), jnp.zeros_like(x)], axis=0)


def right_rows(x):
    a, b, c = split3(x)
    return jnp.concatenate([a, b, a, b, c, a, norm_rows(x, True), jnp.zeros_like(x)], axis=0)


def each(low, high, body):
    for k in range(low, high):
        body(k)


def block_of(left, right, dirs):
    rhs = dirs.shape[0] // 4
    v = jnp.maximum(jnp.dot(left, right, preferred_element_type=F32), 1e-30)
    w = v * lax.rsqrt(v)
    kern = (1.0 + LN2 * w + (LN2 * LN2 / 3.0) * v) * jnp.exp2(-w)
    k1 = kern.astype(BF16)
    k2 = (kern - k1.astype(F32)).astype(BF16)
    total = jnp.dot(dirs, k1, preferred_element_type=F32) + jnp.dot(dirs, k2, preferred_element_type=F32)
    return total[0:rhs] + total[rhs:2 * rhs] + total[2 * rhs:3 * rhs]


def cg_kernel(rows, cols, len_hbm, sig_hbm, noise_hbm, pts_hbm, res_hbm, dir_hbm, move_ref,
              len_ref, sig_ref, noise_ref, pts_ref, res_ref, dir_ref, row_all, col_all, parts, images, sums, in_sem,
              row_send, row_recv, col_send, col_recv, part_send, part_recv, sum_send, sum_recv):
    my_row, my_col = lax.axis_index("row"), lax.axis_index("col")
    dims, width = pts_ref.shape
    rhs = res_ref.shape[0]

    def along(k):
        return (my_row, lax.rem(my_col + k, cols))

    def across(k):
        return (lax.rem(my_row + k, rows), my_col)

    mine_in = [
        pltpu.make_async_copy(pts_hbm, pts_ref, in_sem.at[0]),
        pltpu.make_async_copy(dir_hbm, dir_ref, in_sem.at[1]),
        pltpu.make_async_copy(res_hbm, res_ref, in_sem.at[2]),
        pltpu.make_async_copy(len_hbm, len_ref, in_sem.at[3]),
        pltpu.make_async_copy(sig_hbm, sig_ref, in_sem.at[4]),
        pltpu.make_async_copy(noise_hbm, noise_ref, in_sem.at[5]),
    ]
    for copy in mine_in:
        copy.start()

    barrier = pltpu.get_barrier_semaphore()
    each(1, cols, lambda k: pl.semaphore_signal(
        barrier, inc=1, device_id=along(k), device_id_type=MESH))
    each(1, rows, lambda k: pl.semaphore_signal(
        barrier, inc=1, device_id=across(k), device_id_type=MESH))
    for copy in mine_in[0:3]:
        copy.wait()
    row_all[my_col, :, 0:width] = pts_ref[0:rhs]
    row_all[my_col, :, width:2 * width] = pts_ref[rhs:dims]
    row_all[my_col, :, 2 * width:] = dir_ref[...]
    col_all[my_row, :, 0:width] = pts_ref[0:rhs]
    col_all[my_row, :, width:2 * width] = pts_ref[rhs:dims]
    col_all[my_row, :, 2 * width:3 * width] = dir_ref[...]
    col_all[my_row, :, 3 * width:] = res_ref[...]
    pl.semaphore_wait(barrier, cols - 1 + rows - 1)

    def share(ref, slot, send_sem, recv_sem, peer):
        pltpu.make_async_remote_copy(
            src_ref=ref.at[slot], dst_ref=ref.at[slot], send_sem=send_sem, recv_sem=recv_sem,
            device_id=peer, device_id_type=MESH).start()

    def wait_bytes(ref, sem):
        count = ref.shape[0] - 1
        pltpu.make_async_copy(ref.at[pl.ds(0, count)], ref.at[pl.ds(0, count)], sem).wait()

    each(1, cols, lambda k: share(row_all, my_col, row_send, row_recv, along(k)))
    each(1, rows, lambda k: share(col_all, my_row, col_send, col_recv, across(k)))

    for copy in mine_in[3:]:
        copy.wait()
    row = lax.broadcasted_iota(jnp.int32, (dims, width), 0)
    scale = jnp.zeros((dims, width), F32)
    for i in range(dims):
        scale = jnp.where(row == i, len_ref[i], scale)
    scale = STEP / scale

    def points_of(block):
        return jnp.concatenate([block[:, 0:width], block[:, width:2 * width]], axis=0) * scale

    wait_bytes(col_all, col_recv)
    right = jnp.concatenate([right_rows(points_of(col_all[j])) for j in range(rows)], axis=1).astype(BF16)
    wait_bytes(row_all, row_recv)

    def from_slots(first):
        left, dirs = [], []
        for j in range(group):
            block = row_all[first + j]
            left.append(left_rows(points_of(block)))
            dirs.append(block[:, 2 * width:3 * width])
        left = jnp.concatenate(left, axis=1).T.astype(BF16)
        d1, d2, d3 = split3(jnp.concatenate(dirs, axis=1))
        dirs = jnp.concatenate([d1, d2, d3, jnp.zeros_like(d1)], axis=0).astype(BF16)
        return block_of(left, right, dirs)

    group = math.gcd(cols, max(1, 8 * 4 // rows))
    if group == cols:
        part = from_slots(0)
    else:
        part = lax.fori_loop(0, cols // group, lambda c, acc: acc + from_slots(c * group),
                             jnp.zeros((rhs, rows * width), F32))
    parts[my_row] = part
    each(1, rows, lambda k: share(parts, my_row, part_send, part_recv, across(k)))

    direction = jnp.concatenate([col_all[j, :, 2 * width:3 * width] for j in range(rows)], axis=1)
    residual = jnp.concatenate([col_all[j, :, 3 * width:] for j in range(rows)], axis=1)
    wait_bytes(parts, part_recv)
    image = sig_ref[0, 0] * jnp.sum(parts[...], axis=0) + noise_ref[0, 0] * direction

    def over(x):
        return jnp.sum(x, axis=1, keepdims=True)

    dq, rr, rq, qq = over(direction * image), over(residual * residual), over(residual * image), over(image * image)
    fits = qq > 1e-30
    near = jnp.where(fits, rq / jnp.where(fits, qq, 1.0), 0.0)
    left_over = residual - near * image
    pq, pp = over(left_over * image), over(left_over * left_over)
    lane = lax.broadcasted_iota(jnp.int32, (rhs, width), 1)
    sub = lax.broadcasted_iota(jnp.int32, (rhs, width), 0)
    mine = jnp.zeros((rhs, width), F32)
    for i, item in enumerate((dq, rr, near, qq, pq, pp)):
        mine = jnp.where(lane == sub + i * rhs, item, mine)
    sums[my_col] = jnp.sum(mine, axis=0, keepdims=True)
    each(1, cols, lambda k: share(sums, my_col, sum_send, sum_recv, along(k)))

    for j in range(rows):
        images[j] = image[:, j * width:(j + 1) * width]
    wait_bytes(row_all, row_send)
    wait_bytes(col_all, col_send)
    wait_bytes(parts, part_send)
    wait_bytes(sums, sum_recv)

    every = sums[:, 0, :]

    def item(i):
        return every if i == 0 else pltpu.roll(every, width - i * rhs, 1)

    whole = jnp.sum(every, axis=0, keepdims=True)
    all_rr = jnp.sum(item(1), axis=0, keepdims=True)
    used = lax.broadcasted_iota(jnp.int32, (1, width), 1) < rhs
    alpha = all_rr / jnp.where(used, whole, 1.0)
    off = alpha - item(2)
    new_rr = jnp.sum(item(5) + off * (off * item(3) - 2.0 * item(4)), axis=0, keepdims=True)
    beta = new_rr / jnp.where(used, all_rr, 1.0)
    diag = lane == sub
    alpha = over(jnp.where(diag, alpha, 0.0))
    beta = over(jnp.where(diag, beta, 0.0))
    move_ref[0] = alpha * dir_ref[...]
    move_ref[1] = alpha * images[my_row]
    move_ref[2] = beta * dir_ref[...]
    wait_bytes(sums, sum_send)


def solution(mesh):
    rows, cols = mesh.shape["row"], mesh.shape["col"]

    def on_device(points, lengthscale, signal_var, noise_var, solution, residual, direction):
        rhs, width = direction.shape
        dims = points.shape[0]
        vmem = pl.BlockSpec(memory_space=pltpu.VMEM)
        hbm = pl.BlockSpec(memory_space=pltpu.HBM)
        move = pl.pallas_call(
            functools.partial(cg_kernel, rows, cols),
            out_shape=jax.ShapeDtypeStruct((3, rhs, width), F32),
            in_specs=[hbm] * 6,
            out_specs=vmem,
            scratch_shapes=[
                pltpu.SMEM((dims,), F32),
                pltpu.SMEM((1, 1), F32),
                pltpu.SMEM((1, 1), F32),
                pltpu.VMEM((dims, width), F32),
                pltpu.VMEM((rhs, width), F32),
                pltpu.VMEM((rhs, width), F32),
                pltpu.VMEM((cols, rhs, 3 * width), F32),
                pltpu.VMEM((rows, rhs, 4 * width), F32),
                pltpu.VMEM((rows, rhs, rows * width), F32),
                pltpu.VMEM((rows, rhs, width), F32),
                pltpu.VMEM((cols, 1, width), F32),
                pltpu.SemaphoreType.DMA((6,)),
            ] + [pltpu.SemaphoreType.DMA] * 8,
            compiler_params=pltpu.CompilerParams(
                collective_id=0, has_side_effects=True, vmem_limit_bytes=60 * 1024 * 1024),
            cost_estimate=pl.CostEstimate(
                flops=2 * 80 * rows * cols * width * width, bytes_accessed=32 * 1024,
                transcendentals=2 * rows * cols * width * width),
        )(lengthscale, signal_var.reshape(1, 1), noise_var.reshape(1, 1), points, residual, direction)
        new_residual = residual - move[1]
        return solution + move[0], new_residual, new_residual + move[2]

    spread = P(None, ("row", "col"))
    return jax.shard_map(
        on_device, mesh=mesh, in_specs=(spread, P(), P(), P(), spread, spread, spread),
        out_specs=(spread, spread, spread), check_vma=False)
```

time: 25.7 us -> 22.3 us (0.87)
  Pallas kernels: 22.3 us -> 18.9 us
    pallas_call x1, Pallas kernels: 22.3 us -> 18.9 us  [on_device(): pl.pallas_call(functools.partial(cg_kernel, rows, cols), out_shape=jax.Sh...]
where the time goes in v3:
time: 22.3 us; the launch traced here: 22.1 us
  Pallas kernels  18.9 us (85%)
  between operations  1.96 us (9%)
  other arithmetic  1.28 us (6%)
    pallas_call x1, Pallas kernels, on_device(): pl.pallas_call(functools.partial(cg_kernel, rows, cols), out_shape=jax.Sh...  18.9 us
    add x1, other arithmetic, on_device(): return (solution + move[0], new_residual, new_residual + move[2])  1.28 us

profile of v3, /device:TPU:0, one launch (start us, length us, event | category | flops | bytes accessed | tf_op | source)
XLA Modules:
  0.0 22.1 jit_solution(8343391052234150508)
XLA Ops:
  1.9 0.0 copy-start
  1.9 0.0 copy-start.1
  1.9 18.9 %shard_map.94 = f32[3,4,128]{2,1,0:T(4,128)} custom-call(f32[8]{0:T(128)} %len_hbm.1, f32[1,1]{1,0:T(1,128)} %bitcast.9.sig_hbm, f32[1,1]{1,0:T(1,128)} %bitcast.10.noise_hbm, f32[8,128]{1,0:T(8,128)} %pts_hbm.1, f32[4,128]{1,0:T(4,128)} %res_hbm.1, f32[4,128]{1,0:T(4,128)} %dir_hbm.1), custom_call_target="tpu_custom_call" | custom-call | flops 83886080 | bytes 32768 | tf_op jit(solution)/shard_map/pallas_call | solution.py:208
  20.8 0.0 copy-done
  20.8 0.0 copy-done.1
  20.9 1.3 %bitcast_add_fusion = (f32[4,128]{1,0:T(4,128)}, f32[4,128]{1,0:T(4,128)}, f32[4,128]{1,0:T(4,128)}) fusion(f32[3,4,128]{2,1,0:T(4,128)} %shard_map.94, f32[4,128]{1,0:T(4,128)S(1)} %copy-done, f32[4,128]{1,0:T(4,128)S(1)} %copy-done.1), kind=kLoop, calls=%fused_computation | loop fusion | flops 1536 | bytes 16384 | tf_op jit(solution)/shard_map/add | solution.py:234
Async XLA Ops:
  1.9 18.9 %copy-start = (f32[4,128]{1,0:T(4,128)S(1)}, f32[4,128]{1,0:T(4,128)}, u32[]{:S(2)}) copy-start(f32[4,128]{1,0:T(4,128)} %res_hbm.1) | copy-start | bytes 6148
  1.9 18.9 %copy-start.1 = (f32[4,128]{1,0:T(4,128)S(1)}, f32[4,128]{1,0:T(4,128)}, u32[]{:S(2)}) copy-start(f32[4,128]{1,0:T(4,128)} %param.11) | copy-start | bytes 6148

commit v4 on v3

--- a/solution.py
+++ b/solution.py
@@ -11,8 +11,8 @@
 MESH = pl.DeviceIdType.MESH
 F32 = jnp.float32
 BF16 = jnp.bfloat16
-LN2 = math.log(2.0)
-STEP = math.sqrt(5.0) / LN2
+STEP = math.sqrt(5.0)
+TILE = 256
 
 
 def split3(x):
@@ -52,13 +52,22 @@
 
 def block_of(left, right, dirs):
     rhs = dirs.shape[0] // 4
-    v = jnp.maximum(jnp.dot(left, right, preferred_element_type=F32), 1e-30)
-    w = v * lax.rsqrt(v)
-    kern = (1.0 + LN2 * w + (LN2 * LN2 / 3.0) * v) * jnp.exp2(-w)
-    k1 = kern.astype(BF16)
-    k2 = (kern - k1.astype(F32)).astype(BF16)
-    total = jnp.dot(dirs, k1, preferred_element_type=F32) + jnp.dot(dirs, k2, preferred_element_type=F32)
-    return total[0:rhs] + total[rhs:2 * rhs] + total[2 * rhs:3 * rhs]
+    deep, wide = min(128, left.shape[0]), min(TILE, right.shape[1])
+    out = []
+    for j in range(0, right.shape[1], wide):
+        total = jnp.zeros((dirs.shape[0], wide), F32)
+        for i in range(0, left.shape[0], deep):
+            v = jnp.dot(left[i:i + deep], right[:, j:j + wide], preferred_element_type=F32)
+            v = jnp.maximum(v, 1e-30)
+            t = v * lax.rsqrt(v)
+            kern = (1.0 + t + (1.0 / 3.0) * v) * jnp.exp(-t)
+            k1 = kern.astype(BF16)
+            k2 = (kern - k1.astype(F32)).astype(BF16)
+            rows = dirs[:, i:i + deep]
+            total += jnp.dot(rows, k1, preferred_element_type=F32)
+            total += jnp.dot(rows, k2, preferred_element_type=F32)
+        out.append(total[0:rhs] + total[rhs:2 * rhs] + total[2 * rhs:3 * rhs])
+    return jnp.concatenate(out, axis=1)
 
 
 def cg_kernel(rows, cols, len_hbm, sig_hbm, noise_hbm, pts_hbm, res_hbm, dir_hbm, move_ref,

time: 22.3 us -> 22.2 us (level)
  no operation moved by 1% of the time
where the time goes in v4:
time: 22.2 us; the launch traced here: 22 us
  Pallas kernels  18.7 us (84%)
  between operations  1.96 us (9%)
  other arithmetic  1.28 us (6%)
    pallas_call x1, Pallas kernels, on_device(): pl.pallas_call(functools.partial(cg_kernel, rows, cols), out_shape=jax.Sh...  18.7 us
    add x1, other arithmetic, on_device(): return (solution + move[0], new_residual, new_residual + move[2])  1.28 us

profile of v4, /device:TPU:0, one launch (start us, length us, event | category | flops | bytes accessed | tf_op | source)
XLA Modules:
  0.0 22.0 jit_solution(5844310485298712676)
XLA Ops:
  1.9 0.0 copy-start
  1.9 0.0 copy-start.1
  1.9 18.7 %shard_map.94 = f32[3,4,128]{2,1,0:T(4,128)} custom-call(f32[8]{0:T(128)} %len_hbm.1, f32[1,1]{1,0:T(1,128)} %bitcast.9.sig_hbm, f32[1,1]{1,0:T(1,128)} %bitcast.10.noise_hbm, f32[8,128]{1,0:T(8,128)} %pts_hbm.1, f32[4,128]{1,0:T(4,128)} %res_hbm.1, f32[4,128]{1,0:T(4,128)} %dir_hbm.1), custom_call_target="tpu_custom_call" | custom-call | flops 83886080 | bytes 32768 | tf_op jit(solution)/shard_map/pallas_call | solution.py:217
  20.7 0.0 copy-done
  20.7 0.0 copy-done.1
  20.7 1.3 %bitcast_add_fusion = (f32[4,128]{1,0:T(4,128)}, f32[4,128]{1,0:T(4,128)}, f32[4,128]{1,0:T(4,128)}) fusion(f32[3,4,128]{2,1,0:T(4,128)} %shard_map.94, f32[4,128]{1,0:T(4,128)S(1)} %copy-done, f32[4,128]{1,0:T(4,128)S(1)} %copy-done.1), kind=kLoop, calls=%fused_computation | loop fusion | flops 1536 | bytes 16384 | tf_op jit(solution)/shard_map/add | solution.py:243
Async XLA Ops:
  1.9 18.8 %copy-start = (f32[4,128]{1,0:T(4,128)S(1)}, f32[4,128]{1,0:T(4,128)}, u32[]{:S(2)}) copy-start(f32[4,128]{1,0:T(4,128)} %res_hbm.1) | copy-start | bytes 6148
  1.9 18.8 %copy-start.1 = (f32[4,128]{1,0:T(4,128)S(1)}, f32[4,128]{1,0:T(4,128)}, u32[]{:S(2)}) copy-start(f32[4,128]{1,0:T(4,128)} %param.11) | copy-start | bytes 6148

commit v5 on v4

--- a/solution.py
+++ b/solution.py
@@ -50,14 +50,12 @@
         body(k)
 
 
-def block_of(left, right, dirs):
-    rhs = dirs.shape[0] // 4
-    deep, wide = min(128, left.shape[0]), min(TILE, right.shape[1])
+def add_block(totals, left, right, dirs):
+    deep, wide = min(128, left.shape[0]), right.shape[1] // len(totals)
     out = []
-    for j in range(0, right.shape[1], wide):
-        total = jnp.zeros((dirs.shape[0], wide), F32)
+    for j, total in enumerate(totals):
         for i in range(0, left.shape[0], deep):
-            v = jnp.dot(left[i:i + deep], right[:, j:j + wide], preferred_element_type=F32)
+            v = jnp.dot(left[i:i + deep], right[:, j * wide:(j + 1) * wide], preferred_element_type=F32)
             v = jnp.maximum(v, 1e-30)
             t = v * lax.rsqrt(v)
             kern = (1.0 + t + (1.0 / 3.0) * v) * jnp.exp(-t)
@@ -66,8 +64,8 @@
             rows = dirs[:, i:i + deep]
             total += jnp.dot(rows, k1, preferred_element_type=F32)
             total += jnp.dot(rows, k2, preferred_element_type=F32)
-        out.append(total[0:rhs] + total[rhs:2 * rhs] + total[2 * rhs:3 * rhs])
-    return jnp.concatenate(out, axis=1)
+        out.append(total)
+    return out
 
 
 def cg_kernel(rows, cols, len_hbm, sig_hbm, noise_hbm, pts_hbm, res_hbm, dir_hbm, move_ref,
@@ -77,8 +75,17 @@
     dims, width = pts_ref.shape
     rhs = res_ref.shape[0]
 
+    def partner(k):
+        if cols & (cols - 1):
+            return lax.rem(my_col + k, cols), lax.rem(my_col + cols - k, cols)
+        peer = my_col
+        for b in range(cols.bit_length()):
+            if (k >> b) & 1:
+                peer = peer + (1 << b) - (2 << b) * lax.rem(my_col // (1 << b), 2)
+        return peer, peer
+
     def along(k):
-        return (my_row, lax.rem(my_col + k, cols))
+        return (my_row, partner(k)[0])
 
     def across(k):
         return (lax.rem(my_row + k, rows), my_col)
@@ -91,14 +98,14 @@
         pltpu.make_async_copy(sig_hbm, sig_ref, in_sem.at[4]),
         pltpu.make_async_copy(noise_hbm, noise_ref, in_sem.at[5]),
     ]
-    for copy in mine_in:
-        copy.start()
 
     barrier = pltpu.get_barrier_semaphore()
     each(1, cols, lambda k: pl.semaphore_signal(
         barrier, inc=1, device_id=along(k), device_id_type=MESH))
     each(1, rows, lambda k: pl.semaphore_signal(
         barrier, inc=1, device_id=across(k), device_id_type=MESH))
+    for copy in mine_in:
+        copy.start()
     for copy in mine_in[0:3]:
         copy.wait()
     row_all[my_col, :, 0:width] = pts_ref[0:rhs]
@@ -119,8 +126,8 @@
         count = ref.shape[0] - 1
         pltpu.make_async_copy(ref.at[pl.ds(0, count)], ref.at[pl.ds(0, count)], sem).wait()
 
-    each(1, cols, lambda k: share(row_all, my_col, row_send, row_recv, along(k)))
     each(1, rows, lambda k: share(col_all, my_row, col_send, col_recv, across(k)))
+    each(1, cols, lambda k: share(row_all, my_col, row_send, row_recv.at[k], along(k)))
 
     for copy in mine_in[3:]:
         copy.wait()
@@ -135,47 +142,46 @@
 
     wait_bytes(col_all, col_recv)
     right = jnp.concatenate([right_rows(points_of(col_all[j])) for j in range(rows)], axis=1).astype(BF16)
-    wait_bytes(row_all, row_recv)
-
-    def from_slots(first):
+
+    tiles = max(1, right.shape[1] // TILE)
+    totals = [jnp.zeros((4 * rhs, right.shape[1] // tiles), F32)] * tiles
+    pair = math.gcd(cols, 2)
+    for first in range(0, cols, pair):
         left, dirs = [], []
-        for j in range(group):
-            block = row_all[first + j]
+        for k in range(first, first + pair):
+            source = partner(k)[1]
+            if k > 0:
+                pltpu.make_async_copy(row_all.at[source], row_all.at[source], row_recv.at[k]).wait()
+            block = row_all[source]
             left.append(left_rows(points_of(block)))
             dirs.append(block[:, 2 * width:3 * width])
         left = jnp.concatenate(left, axis=1).T.astype(BF16)
         d1, d2, d3 = split3(jnp.concatenate(dirs, axis=1))
         dirs = jnp.concatenate([d1, d2, d3, jnp.zeros_like(d1)], axis=0).astype(BF16)
-        return block_of(left, right, dirs)
-
-    group = math.gcd(cols, max(1, 8 * 4 // rows))
-    if group == cols:
-        part = from_slots(0)
-    else:
-        part = lax.fori_loop(0, cols // group, lambda c, acc: acc + from_slots(c * group),
-                             jnp.zeros((rhs, rows * width), F32))
+        totals = add_block(totals, left, right, dirs)
+    part = jnp.concatenate([t[0:rhs] + t[rhs:2 * rhs] + t[2 * rhs:3 * rhs] for t in totals], axis=1)
     parts[my_row] = part
     each(1, rows, lambda k: share(parts, my_row, part_send, part_recv, across(k)))
 
+    def over(x):
+        return jnp.sum(x, axis=1, keepdims=True)
+
     direction = jnp.concatenate([col_all[j, :, 2 * width:3 * width] for j in range(rows)], axis=1)
     residual = jnp.concatenate([col_all[j, :, 3 * width:] for j in range(rows)], axis=1)
+    rr = over(residual * residual)
     wait_bytes(parts, part_recv)
     image = sig_ref[0, 0] * jnp.sum(parts[...], axis=0) + noise_ref[0, 0] * direction
 
-    def over(x):
-        return jnp.sum(x, axis=1, keepdims=True)
-
-    dq, rr, rq, qq = over(direction * image), over(residual * residual), over(residual * image), over(image * image)
+    dq, rq, qq = over(direction * image), over(residual * image), over(image * image)
     fits = qq > 1e-30
     near = jnp.where(fits, rq / jnp.where(fits, qq, 1.0), 0.0)
     left_over = residual - near * image
     pq, pp = over(left_over * image), over(left_over * left_over)
     lane = lax.broadcasted_iota(jnp.int32, (rhs, width), 1)
-    sub = lax.broadcasted_iota(jnp.int32, (rhs, width), 0)
     mine = jnp.zeros((rhs, width), F32)
     for i, item in enumerate((dq, rr, near, qq, pq, pp)):
-        mine = jnp.where(lane == sub + i * rhs, item, mine)
-    sums[my_col] = jnp.sum(mine, axis=0, keepdims=True)
+        mine = jnp.where(lane == i, item, mine)
+    sums[my_col] = mine
     each(1, cols, lambda k: share(sums, my_col, sum_send, sum_recv, along(k)))
 
     for j in range(rows):
@@ -185,21 +191,24 @@
     wait_bytes(parts, part_send)
     wait_bytes(sums, sum_recv)
 
-    every = sums[:, 0, :]
+    def total_of(x):
+        out = x[0:rhs]
+        for j in range(1, cols):
+            out = out + x[j * rhs:(j + 1) * rhs]
+        return out
+
+    every = jnp.concatenate([sums[j] for j in range(cols)], axis=0)
 
     def item(i):
-        return every if i == 0 else pltpu.roll(every, width - i * rhs, 1)
-
-    whole = jnp.sum(every, axis=0, keepdims=True)
-    all_rr = jnp.sum(item(1), axis=0, keepdims=True)
-    used = lax.broadcasted_iota(jnp.int32, (1, width), 1) < rhs
-    alpha = all_rr / jnp.where(used, whole, 1.0)
-    off = alpha - item(2)
-    new_rr = jnp.sum(item(5) + off * (off * item(3) - 2.0 * item(4)), axis=0, keepdims=True)
-    beta = new_rr / jnp.where(used, all_rr, 1.0)
-    diag = lane == sub
-    alpha = over(jnp.where(diag, alpha, 0.0))
-    beta = over(jnp.where(diag, beta, 0.0))
+        return every if i == 0 else pltpu.roll(every, width - i, 1)
+
+    used = lane == 0
+    all_rr = jnp.where(used, total_of(item(1)), 1.0)
+    alpha = all_rr / jnp.where(used, total_of(every), 1.0)
+    off = jnp.concatenate([alpha] * cols, axis=0) - item(2)
+    new_rr = total_of(item(5) + off * (off * item(3) - 2.0 * item(4)))
+    beta = new_rr / all_rr
+    alpha, beta = alpha[:, 0:1], beta[:, 0:1]
     move_ref[0] = alpha * dir_ref[...]
     move_ref[1] = alpha * images[my_row]
     move_ref[2] = beta * dir_ref[...]
@@ -230,9 +239,11 @@
                 pltpu.VMEM((rows, rhs, 4 * width), F32),
                 pltpu.VMEM((rows, rhs, rows * width), F32),
                 pltpu.VMEM((rows, rhs, width), F32),
-                pltpu.VMEM((cols, 1, width), F32),
+                pltpu.VMEM((cols, rhs, width), F32),
                 pltpu.SemaphoreType.DMA((6,)),
-            ] + [pltpu.SemaphoreType.DMA] * 8,
+                pltpu.SemaphoreType.DMA,
+                pltpu.SemaphoreType.DMA((cols,)),
+            ] + [pltpu.SemaphoreType.DMA] * 6,
             compiler_params=pltpu.CompilerParams(
                 collective_id=0, has_side_effects=True, vmem_limit_bytes=60 * 1024 * 1024),
             cost_estimate=pl.CostEstimate(

time: 22.2 us -> 22 us (level)
  no operation moved by 1% of the time
where the time goes in v5:
time: 22 us; the launch traced here: 21.9 us
  Pallas kernels  18.6 us (85%)
  between operations  1.96 us (9%)
  other arithmetic  1.28 us (6%)
    pallas_call x1, Pallas kernels, on_device(): pl.pallas_call(functools.partial(cg_kernel, rows, cols), out_shape=jax.Sh...  18.6 us
    add x1, other arithmetic, on_device(): return (solution + move[0], new_residual, new_residual + move[2])  1.28 us

profile of v5, /device:TPU:0, one launch (start us, length us, event | category | flops | bytes accessed | tf_op | source)
XLA Modules:
  0.0 21.9 jit_solution(17654069927882607376)
XLA Ops:
  1.9 0.0 copy-start
  1.9 0.0 copy-start.1
  1.9 18.6 %shard_map.94 = f32[3,4,128]{2,1,0:T(4,128)} custom-call(f32[8]{0:T(128)} %len_hbm.1, f32[1,1]{1,0:T(1,128)} %bitcast.9.sig_hbm, f32[1,1]{1,0:T(1,128)} %bitcast.10.noise_hbm, f32[8,128]{1,0:T(8,128)} %pts_hbm.1, f32[4,128]{1,0:T(4,128)} %res_hbm.1, f32[4,128]{1,0:T(4,128)} %dir_hbm.1), custom_call_target="tpu_custom_call" | custom-call | flops 83886080 | bytes 32768 | tf_op jit(solution)/shard_map/pallas_call | solution.py:226
  20.6 0.0 copy-done
  20.6 0.0 copy-done.1
  20.6 1.3 %bitcast_add_fusion = (f32[4,128]{1,0:T(4,128)}, f32[4,128]{1,0:T(4,128)}, f32[4,128]{1,0:T(4,128)}) fusion(f32[3,4,128]{2,1,0:T(4,128)} %shard_map.94, f32[4,128]{1,0:T(4,128)S(1)} %copy-done, f32[4,128]{1,0:T(4,128)S(1)} %copy-done.1), kind=kLoop, calls=%fused_computation | loop fusion | flops 1536 | bytes 16384 | tf_op jit(solution)/shard_map/add | solution.py:254
Async XLA Ops:
  1.9 18.6 %copy-start = (f32[4,128]{1,0:T(4,128)S(1)}, f32[4,128]{1,0:T(4,128)}, u32[]{:S(2)}) copy-start(f32[4,128]{1,0:T(4,128)} %res_hbm.1) | copy-start | bytes 6148
  1.9 18.6 %copy-start.1 = (f32[4,128]{1,0:T(4,128)S(1)}, f32[4,128]{1,0:T(4,128)}, u32[]{:S(2)}) copy-start(f32[4,128]{1,0:T(4,128)} %param.11) | copy-start | bytes 6148

commit v6 on v5

--- a/solution.py
+++ b/solution.py
@@ -68,8 +68,8 @@
     return out
 
 
-def cg_kernel(rows, cols, len_hbm, sig_hbm, noise_hbm, pts_hbm, res_hbm, dir_hbm, move_ref,
-              len_ref, sig_ref, noise_ref, pts_ref, res_ref, dir_ref, row_all, col_all, parts, images, sums, in_sem,
+def cg_kernel(rows, cols, len_hbm, sig_hbm, noise_hbm, pts_ref, res_ref, dir_ref, move_ref,
+              len_ref, sig_ref, noise_ref, row_all, col_all, parts, images, sums, in_sem,
               row_send, row_recv, col_send, col_recv, part_send, part_recv, sum_send, sum_recv):
     my_row, my_col = lax.axis_index("row"), lax.axis_index("col")
     dims, width = pts_ref.shape
@@ -91,12 +91,9 @@
         return (lax.rem(my_row + k, rows), my_col)
 
     mine_in = [
-        pltpu.make_async_copy(pts_hbm, pts_ref, in_sem.at[0]),
-        pltpu.make_async_copy(dir_hbm, dir_ref, in_sem.at[1]),
-        pltpu.make_async_copy(res_hbm, res_ref, in_sem.at[2]),
-        pltpu.make_async_copy(len_hbm, len_ref, in_sem.at[3]),
-        pltpu.make_async_copy(sig_hbm, sig_ref, in_sem.at[4]),
-        pltpu.make_async_copy(noise_hbm, noise_ref, in_sem.at[5]),
+        pltpu.make_async_copy(len_hbm, len_ref, in_sem.at[0]),
+        pltpu.make_async_copy(sig_hbm, sig_ref, in_sem.at[1]),
+        pltpu.make_async_copy(noise_hbm, noise_ref, in_sem.at[2]),
     ]
 
     barrier = pltpu.get_barrier_semaphore()
@@ -106,8 +103,6 @@
         barrier, inc=1, device_id=across(k), device_id_type=MESH))
     for copy in mine_in:
         copy.start()
-    for copy in mine_in[0:3]:
-        copy.wait()
     row_all[my_col, :, 0:width] = pts_ref[0:rhs]
     row_all[my_col, :, width:2 * width] = pts_ref[rhs:dims]
     row_all[my_col, :, 2 * width:] = dir_ref[...]
@@ -129,7 +124,7 @@
     each(1, rows, lambda k: share(col_all, my_row, col_send, col_recv, across(k)))
     each(1, cols, lambda k: share(row_all, my_col, row_send, row_recv.at[k], along(k)))
 
-    for copy in mine_in[3:]:
+    for copy in mine_in:
         copy.wait()
     row = lax.broadcasted_iota(jnp.int32, (dims, width), 0)
     scale = jnp.zeros((dims, width), F32)
@@ -226,26 +221,23 @@
         move = pl.pallas_call(
             functools.partial(cg_kernel, rows, cols),
             out_shape=jax.ShapeDtypeStruct((3, rhs, width), F32),
-            in_specs=[hbm] * 6,
+            in_specs=[hbm] * 3 + [vmem] * 3,
             out_specs=vmem,
             scratch_shapes=[
                 pltpu.SMEM((dims,), F32),
                 pltpu.SMEM((1, 1), F32),
                 pltpu.SMEM((1, 1), F32),
-                pltpu.VMEM((dims, width), F32),
-                pltpu.VMEM((rhs, width), F32),
-                pltpu.VMEM((rhs, width), F32),
                 pltpu.VMEM((cols, rhs, 3 * width), F32),
                 pltpu.VMEM((rows, rhs, 4 * width), F32),
                 pltpu.VMEM((rows, rhs, rows * width), F32),
                 pltpu.VMEM((rows, rhs, width), F32),
                 pltpu.VMEM((cols, rhs, width), F32),
-                pltpu.SemaphoreType.DMA((6,)),
+                pltpu.SemaphoreType.DMA((3,)),
                 pltpu.SemaphoreType.DMA,
                 pltpu.SemaphoreType.DMA((cols,)),
             ] + [pltpu.SemaphoreType.DMA] * 6,
             compiler_params=pltpu.CompilerParams(
-                collective_id=0, has_side_effects=True, vmem_limit_bytes=60 * 1024 * 1024),
+                collective_id=0, has_side_effects=True, vmem_limit_bytes=32 * 1024 * 1024),
             cost_estimate=pl.CostEstimate(
                 flops=2 * 80 * rows * cols * width * width, bytes_accessed=32 * 1024,
                 transcendentals=2 * rows * cols * width * width),

time: 22 us -> 22 us (level)
  local copies, waits for them, and re-layouts: 0.01 us -> 1.32 us
  Pallas kernels: 18.6 us -> 17.9 us
  other arithmetic: 1.28 us -> 0.59 us
    unnamed x4 -> x10, local copies, waits for them, and re-layouts: 0.01 us -> 1.32 us
    pallas_call x1, Pallas kernels: 18.6 us -> 17.9 us  [on_device(): pl.pallas_call(functools.partial(cg_kernel, rows, cols), out_shape=jax.Sh...]
    add x1, other arithmetic: 1.28 us -> 0.59 us  [on_device(): return (solution + move[0], new_residual, new_residual + move[2])]
where the time goes in v6:
time: 22 us; the launch traced here: 21.8 us
  Pallas kernels  17.9 us (81%)
  between operations  2.01 us (9%)
  local copies, waits for them, and re-layouts  1.32 us (6%)
  other arithmetic  0.59 us (3%)
    pallas_call x1, Pallas kernels, on_device(): pl.pallas_call(functools.partial(cg_kernel, rows, cols), out_shape=jax.Sh...  17.9 us
    unnamed x10, local copies, waits for them, and re-layouts  1.32 us
    add x1, other arithmetic, on_device(): return (solution + move[0], new_residual, new_residual + move[2])  0.59 us

profile of v6, /device:TPU:0, one launch (start us, length us, event | category | flops | bytes accessed | tf_op | source)
XLA Modules:
  0.0 21.8 jit_solution(16233584347746317242)
XLA Ops:
  0.6 0.0 copy-start.1
  1.3 0.0 copy-start
  2.0 0.0 copy-start.3
  2.0 0.0 copy-done.1
  2.0 0.0 copy-done
  2.0 0.6 %copy-done.3 = f32[8]{0:T(128)S(1)} copy-done((f32[8]{0:T(128)S(1)}, f32[8]{0:T(128)}, u32[]{:S(2)}) %copy-start.3) | copy-done | bytes 56
  2.6 0.0 copy-start.2
  2.6 0.7 %copy-done.2 = f32[4,128]{1,0:T(4,128)S(1)} copy-done((f32[4,128]{1,0:T(4,128)S(1)}, f32[4,128]{1,0:T(4,128)}, u32[]{:S(2)}) %copy-start.2) | copy-done | bytes 2072
  3.3 0.0 copy-start.4
  3.3 17.9 %shard_map.94 = f32[3,4,128]{2,1,0:T(4,128)S(1)} custom-call(f32[8]{0:T(128)S(1)} %copy-done.3, f32[1,1]{1,0:T(1,128)} %bitcast.9.sig_hbm, f32[1,1]{1,0:T(1,128)} %bitcast.10.noise_hbm, f32[8,128]{1,0:T(8,128)S(1)} %copy-done.1, f32[4,128]{1,0:T(4,128)S(1)} %copy-done, f32[4,128]{1,0:T(4,128)S(1)} %copy-done.2), custom_call_target="tpu_custom_call" | custom-call | flops 83886080 | bytes 32768 | tf_op jit(solution)/shard_map/pallas_call | solution.py:221
  21.2 0.0 copy-done.4
  21.2 0.6 %bitcast_add_fusion = (f32[4,128]{1,0:T(4,128)}, f32[4,128]{1,0:T(4,128)}, f32[4,128]{1,0:T(4,128)}) fusion(f32[3,4,128]{2,1,0:T(4,128)S(1)} %shard_map.94, f32[4,128]{1,0:T(4,128)S(1)} %copy-done, f32[4,128]{1,0:T(4,128)S(1)} %copy-done.4), kind=kLoop, calls=%fused_computation | loop fusion | flops 1536 | bytes 16384 | tf_op jit(solution)/shard_map/add | solution.py:246
Async XLA Ops:
  0.6 1.3 %copy-start.1 = (f32[8,128]{1,0:T(8,128)S(1)}, f32[8,128]{1,0:T(8,128)}, u32[]{:S(2)}) copy-start(f32[8,128]{1,0:T(8,128)} %pts_ref.1) | copy-start | bytes 12292
  1.3 0.7 %copy-start = (f32[4,128]{1,0:T(4,128)S(1)}, f32[4,128]{1,0:T(4,128)}, u32[]{:S(2)}) copy-start(f32[4,128]{1,0:T(4,128)} %res_ref.1) | copy-start | bytes 6148
  2.0 0.7 %copy-start.3 = (f32[8]{0:T(128)S(1)}, f32[8]{0:T(128)}, u32[]{:S(2)}) copy-start(f32[8]{0:T(128)} %len_hbm.1) | copy-start | bytes 100
  2.6 0.7 %copy-start.2 = (f32[4,128]{1,0:T(4,128)S(1)}, f32[4,128]{1,0:T(4,128)}, u32[]{:S(2)}) copy-start(f32[4,128]{1,0:T(4,128)} %dir_ref.1) | copy-start | bytes 6148
  3.3 17.9 %copy-start.4 = (f32[4,128]{1,0:T(4,128)S(1)}, f32[4,128]{1,0:T(4,128)}, u32[]{:S(2)}) copy-start(f32[4,128]{1,0:T(4,128)} %param.11) | copy-start | bytes 6148

commit v7 on v6

--- a/solution.py
+++ b/solution.py
@@ -129,7 +129,7 @@
     row = lax.broadcasted_iota(jnp.int32, (dims, width), 0)
     scale = jnp.zeros((dims, width), F32)
     for i in range(dims):
-        scale = jnp.where(row == i, len_ref[i], scale)
+        scale = jnp.where(row == i, len_ref[0, i], scale)
     scale = STEP / scale
 
     def points_of(block):
@@ -224,7 +224,7 @@
             in_specs=[hbm] * 3 + [vmem] * 3,
             out_specs=vmem,
             scratch_shapes=[
-                pltpu.SMEM((dims,), F32),
+                pltpu.SMEM((1, dims), F32),
                 pltpu.SMEM((1, 1), F32),
                 pltpu.SMEM((1, 1), F32),
                 pltpu.VMEM((cols, rhs, 3 * width), F32),
@@ -241,7 +241,7 @@
             cost_estimate=pl.CostEstimate(
                 flops=2 * 80 * rows * cols * width * width, bytes_accessed=32 * 1024,
                 transcendentals=2 * rows * cols * width * width),
-        )(lengthscale, signal_var.reshape(1, 1), noise_var.reshape(1, 1), points, residual, direction)
+        )(lengthscale.reshape(1, -1), signal_var.reshape(1, 1), noise_var.reshape(1, 1), points, residual, direction)
         new_residual = residual - move[1]
         return solution + move[0], new_residual, new_residual + move[2]
 

time: 22 us -> 21.4 us (0.973)
  local copies, waits for them, and re-layouts: 1.32 us -> 0.66 us
    unnamed x10, local copies, waits for them, and re-layouts: 1.32 us -> 0.66 us
where the time goes in v7:
time: 21.4 us; the launch traced here: 21.2 us
  Pallas kernels  17.9 us (84%)
  between operations  2.01 us (9%)
  local copies, waits for them, and re-layouts  0.66 us (3%)
  other arithmetic  0.59 us (3%)
    pallas_call x1, Pallas kernels, on_device(): pl.pallas_call(functools.partial(cg_kernel, rows, cols), out_shape=jax.Sh...  17.9 us
    unnamed x10, local copies, waits for them, and re-layouts  0.66 us
    add x1, other arithmetic, on_device(): return (solution + move[0], new_residual, new_residual + move[2])  0.59 us

profile of v7, /device:TPU:0, one launch (start us, length us, event | category | flops | bytes accessed | tf_op | source)
XLA Modules:
  0.0 21.2 jit_solution(14764336280543038685)
XLA Ops:
  0.6 0.0 copy-start.2
  1.3 0.0 copy-start.1
  2.0 0.0 copy-start
  2.0 0.0 copy-start.3
  2.0 0.0 copy-done.2
  2.0 0.0 copy-done.1
  2.0 0.6 %copy-done = f32[4,128]{1,0:T(4,128)S(1)} copy-done((f32[4,128]{1,0:T(4,128)S(1)}, f32[4,128]{1,0:T(4,128)}, u32[]{:S(2)}) %copy-start) | copy-done | bytes 2072
  2.7 0.0 copy-done.3
  2.7 0.0 copy-start.4
  2.7 17.9 %shard_map.94 = f32[3,4,128]{2,1,0:T(4,128)S(1)} custom-call(f32[1,8]{1,0:T(1,128)S(1)} %bitcast.12, f32[1,1]{1,0:T(1,128)} %bitcast.10.sig_hbm, f32[1,1]{1,0:T(1,128)} %bitcast.11.noise_hbm, f32[8,128]{1,0:T(8,128)S(1)} %copy-done.1, f32[4,128]{1,0:T(4,128)S(1)} %copy-done, f32[4,128]{1,0:T(4,128)S(1)} %copy-done.2), custom_call_target="tpu_custom_call" | custom-call | flops 83886080 | bytes 32768 | tf_op jit(solution)/shard_map/pallas_call | solution.py:221
  20.6 0.0 copy-done.4
  20.6 0.6 %bitcast_add_fusion = (f32[4,128]{1,0:T(4,128)}, f32[4,128]{1,0:T(4,128)}, f32[4,128]{1,0:T(4,128)}) fusion(f32[3,4,128]{2,1,0:T(4,128)S(1)} %shard_map.94, f32[4,128]{1,0:T(4,128)S(1)} %copy-done, f32[4,128]{1,0:T(4,128)S(1)} %copy-done.4), kind=kLoop, calls=%fused_computation | loop fusion | flops 1536 | bytes 16384 | tf_op jit(solution)/shard_map/add | solution.py:246
Async XLA Ops:
  0.6 1.4 %copy-start.2 = (f32[4,128]{1,0:T(4,128)S(1)}, f32[4,128]{1,0:T(4,128)}, u32[]{:S(2)}) copy-start(f32[4,128]{1,0:T(4,128)} %dir_ref.1) | copy-start | bytes 6148
  1.3 0.7 %copy-start.1 = (f32[8,128]{1,0:T(8,128)S(1)}, f32[8,128]{1,0:T(8,128)}, u32[]{:S(2)}) copy-start(f32[8,128]{1,0:T(8,128)} %pts_ref.1) | copy-start | bytes 12292
  2.0 0.7 %copy-start = (f32[4,128]{1,0:T(4,128)S(1)}, f32[4,128]{1,0:T(4,128)}, u32[]{:S(2)}) copy-start(f32[4,128]{1,0:T(4,128)} %res_ref.1) | copy-start | bytes 6148
  2.0 0.7 %copy-start.3 = (f32[8]{0:T(128)S(1)}, f32[8]{0:T(128)}, u32[]{:S(2)}) copy-start(f32[8]{0:T(128)} %param.8) | copy-start | bytes 100
  2.7 17.9 %copy-start.4 = (f32[4,128]{1,0:T(4,128)S(1)}, f32[4,128]{1,0:T(4,128)}, u32[]{:S(2)}) copy-start(f32[4,128]{1,0:T(4,128)} %param.11) | copy-start | bytes 6148

commit v8 on v7

--- a/solution.py
+++ b/solution.py
@@ -122,7 +122,7 @@
         pltpu.make_async_copy(ref.at[pl.ds(0, count)], ref.at[pl.ds(0, count)], sem).wait()
 
     each(1, rows, lambda k: share(col_all, my_row, col_send, col_recv, across(k)))
-    each(1, cols, lambda k: share(row_all, my_col, row_send, row_recv.at[k], along(k)))
+    each(1, cols, lambda k: share(row_all, my_col, row_send, row_recv.at[cols - k], along(cols - k)))
 
     for copy in mine_in:
         copy.wait()
@@ -140,7 +140,7 @@
 
     tiles = max(1, right.shape[1] // TILE)
     totals = [jnp.zeros((4 * rhs, right.shape[1] // tiles), F32)] * tiles
-    pair = math.gcd(cols, 2)
+    pair = math.gcd(cols, 4)
     for first in range(0, cols, pair):
         left, dirs = [], []
         for k in range(first, first + pair):
@@ -181,9 +181,6 @@
 
     for j in range(rows):
         images[j] = image[:, j * width:(j + 1) * width]
-    wait_bytes(row_all, row_send)
-    wait_bytes(col_all, col_send)
-    wait_bytes(parts, part_send)
     wait_bytes(sums, sum_recv)
 
     def total_of(x):
@@ -207,6 +204,9 @@
     move_ref[0] = alpha * dir_ref[...]
     move_ref[1] = alpha * images[my_row]
     move_ref[2] = beta * dir_ref[...]
+    wait_bytes(row_all, row_send)
+    wait_bytes(col_all, col_send)
+    wait_bytes(parts, part_send)
     wait_bytes(sums, sum_send)
 
 

time: 21.4 us -> 21.1 us (0.986)
  Pallas kernels: 17.9 us -> 17.6 us
    pallas_call x1, Pallas kernels: 17.9 us -> 17.6 us  [on_device(): pl.pallas_call(functools.partial(cg_kernel, rows, cols), out_shape=jax.Sh...]
where the time goes in v8:
time: 21.1 us; the launch traced here: 20.9 us
  Pallas kernels  17.6 us (83%)
  between operations  2.01 us (10%)
  local copies, waits for them, and re-layouts  0.66 us (3%)
  other arithmetic  0.59 us (3%)
    pallas_call x1, Pallas kernels, on_device(): pl.pallas_call(functools.partial(cg_kernel, rows, cols), out_shape=jax.Sh...  17.6 us
    unnamed x10, local copies, waits for them, and re-layouts  0.66 us
    add x1, other arithmetic, on_device(): return (solution + move[0], new_residual, new_residual + move[2])  0.59 us

profile of v8, /device:TPU:0, one launch (start us, length us, event | category | flops | bytes accessed | tf_op | source)
XLA Modules:
  0.0 20.9 jit_solution(16176999041527059248)
XLA Ops:
  0.6 0.0 copy-start.2
  1.3 0.0 copy-start.1
  2.0 0.0 copy-start
  2.0 0.0 copy-start.3
  2.0 0.0 copy-done.2
  2.0 0.0 copy-done.1
  2.0 0.6 %copy-done = f32[4,128]{1,0:T(4,128)S(1)} copy-done((f32[4,128]{1,0:T(4,128)S(1)}, f32[4,128]{1,0:T(4,128)}, u32[]{:S(2)}) %copy-start) | copy-done | bytes 2072
  2.7 0.0 copy-done.3
  2.7 0.0 copy-start.4
  2.7 17.6 %shard_map.94 = f32[3,4,128]{2,1,0:T(4,128)S(1)} custom-call(f32[1,8]{1,0:T(1,128)S(1)} %bitcast.12, f32[1,1]{1,0:T(1,128)} %bitcast.10.sig_hbm, f32[1,1]{1,0:T(1,128)} %bitcast.11.noise_hbm, f32[8,128]{1,0:T(8,128)S(1)} %copy-done.1, f32[4,128]{1,0:T(4,128)S(1)} %copy-done, f32[4,128]{1,0:T(4,128)S(1)} %copy-done.2), custom_call_target="tpu_custom_call" | custom-call | flops 83886080 | bytes 32768 | tf_op jit(solution)/shard_map/pallas_call | solution.py:221
  20.3 0.0 copy-done.4
  20.3 0.6 %bitcast_add_fusion = (f32[4,128]{1,0:T(4,128)}, f32[4,128]{1,0:T(4,128)}, f32[4,128]{1,0:T(4,128)}) fusion(f32[3,4,128]{2,1,0:T(4,128)S(1)} %shard_map.94, f32[4,128]{1,0:T(4,128)S(1)} %copy-done, f32[4,128]{1,0:T(4,128)S(1)} %copy-done.4), kind=kLoop, calls=%fused_computation | loop fusion | flops 1536 | bytes 16384 | tf_op jit(solution)/shard_map/add | solution.py:246
Async XLA Ops:
  0.6 1.4 %copy-start.2 = (f32[4,128]{1,0:T(4,128)S(1)}, f32[4,128]{1,0:T(4,128)}, u32[]{:S(2)}) copy-start(f32[4,128]{1,0:T(4,128)} %dir_ref.1) | copy-start | bytes 6148
  1.3 0.7 %copy-start.1 = (f32[8,128]{1,0:T(8,128)S(1)}, f32[8,128]{1,0:T(8,128)}, u32[]{:S(2)}) copy-start(f32[8,128]{1,0:T(8,128)} %pts_ref.1) | copy-start | bytes 12292
  2.0 0.7 %copy-start = (f32[4,128]{1,0:T(4,128)S(1)}, f32[4,128]{1,0:T(4,128)}, u32[]{:S(2)}) copy-start(f32[4,128]{1,0:T(4,128)} %res_ref.1) | copy-start | bytes 6148
  2.0 0.7 %copy-start.3 = (f32[8]{0:T(128)S(1)}, f32[8]{0:T(128)}, u32[]{:S(2)}) copy-start(f32[8]{0:T(128)} %param.8) | copy-start | bytes 100
  2.7 17.6 %copy-start.4 = (f32[4,128]{1,0:T(4,128)S(1)}, f32[4,128]{1,0:T(4,128)}, u32[]{:S(2)}) copy-start(f32[4,128]{1,0:T(4,128)} %param.11) | copy-start | bytes 6148
